TPU v7x, 128 devices: a whole 4x4x4 slice. The times are simulated.
128 devices in a mesh: row: 8 (over z, x_hi), col: 16 (over y, x_lo, core).
Axes of the slice: x: 4 (x_hi: 2, x_lo: 2; x = x_hi * 2 + x_lo), y: 4, z: 4, core: 2. Of those that a mesh axis runs over, the one named last changes fastest.
Arguments:
- factor: bfloat16 [16384, 16384], P('row', 'col'), may hold values from -1 to 7, as said below
- old_basis: bfloat16 [16384, 2048], P(('col', 'row')), may hold values from -9 to 9, as said below
- first_moment: float32 [16384, 2048], P(('col', 'row')), may hold values from -1.8 to 1.8
Outputs:
- new_basis: bfloat16 [16384, 2048], P(('col', 'row'))
- rotated_moment: float32 [16384, 2048], P(('col', 'row'))
Inputs may be any that keep to these rules, and one draw needn't show every extreme that they name: factor equals its transpose and is positive definite. old_basis has full column rank.
All inputs are finite; a program needn't handle non-finite values.
Results may differ from a plain program's by a relative error of at most 0.0053.
Values may be sent and summed in bfloat16 or wider, within the bound.
A program may use at most 192 MiB of HBM per device.

v0:
```python
import jax
import jax.numpy as jnp
from jax import lax
from jax.sharding import PartitionSpec as P

M = 16384


def blocked_cholesky(gram_matrix):
    width = gram_matrix.shape[0]
    step_width = min(512, width)
    steps_total = width // step_width
    trailing = gram_matrix
    pieces = []
    inverses = []
    for position in range(steps_total):
        head = trailing[:step_width, :step_width]
        diag_factor = jnp.linalg.cholesky(head)
        inverse = jax.scipy.linalg.solve_triangular(
            diag_factor, jnp.eye(step_width, dtype=jnp.float32), lower=True
        )
        below = jnp.dot(
            trailing[step_width:, :step_width], inverse.T, precision=lax.Precision.HIGHEST
        )
        above = jnp.zeros((position * step_width, step_width), jnp.float32)
        pieces.append(jnp.concatenate([above, diag_factor, below], 0))
        inverses.append(inverse)
        trailing = trailing[step_width:, step_width:] - jnp.dot(
            below, below.T, precision=lax.Precision.HIGHEST
        )
    return (jnp.concatenate(pieces, 1), inverses, step_width)


def blocked_solve(lower_factor, inverses, step_width, rhs_matrix):
    solved = []
    for position in range(len(inverses)):
        begin = position * step_width
        current = rhs_matrix[:, begin : begin + step_width]
        if position > 0:
            earlier = jnp.concatenate(solved, 1)
            coupling = lower_factor[begin : begin + step_width, :begin]
            current = current - jnp.dot(earlier, coupling.T, precision=lax.Precision.HIGHEST)
        solved.append(jnp.dot(current, inverses[position].T, precision=lax.Precision.HIGHEST))
    return jnp.concatenate(solved, 1)


def body(factor, old_basis, first_moment):
    grid_rows = lax.axis_size("row")
    grid_columns = lax.axis_size("col")
    tile_rows, tile_columns = factor.shape
    slab_rows, panel_width = old_basis.shape
    groups = grid_columns // grid_rows
    column_panel = lax.all_gather(old_basis, "row", axis=0, tiled=True)
    sub_rows = slab_rows // grid_columns
    arranged = factor.reshape(groups, grid_rows, grid_columns, sub_rows, tile_columns)
    stripe = arranged
    stripe = jnp.transpose(stripe, (2, 1, 0, 3, 4)).reshape(
        lax.axis_size("col") * slab_rows, tile_columns
    )
    summed = lax.psum_scatter(
        jnp.dot(stripe, column_panel, preferred_element_type=jnp.float32),
        "col",
        scatter_dimension=0,
        tiled=True,
    )
    relayed = summed.astype(jnp.bfloat16).reshape(grid_rows, groups, sub_rows, panel_width)
    relayed = lax.all_to_all(relayed, "row", split_axis=0, concat_axis=0, tiled=True)
    relayed = relayed.reshape(grid_columns, sub_rows, panel_width)
    relayed = lax.all_to_all(relayed, "col", split_axis=0, concat_axis=0, tiled=True)
    product = relayed.reshape(slab_rows, panel_width)
    gram_part = lax.dot_general(
        product, product, (((0,), (0,)), ((), ())), preferred_element_type=jnp.float32
    )
    gram_part = gram_part * (1.0 / M)
    gram_matrix = lax.psum(gram_part, ("row", "col"))
    lower_factor, inverses, step_width = blocked_cholesky(gram_matrix)
    solved = blocked_solve(lower_factor, inverses, step_width, product.astype(jnp.float32))
    new_basis = solved.astype(jnp.bfloat16)
    rotated_moment = jnp.dot(first_moment, lower_factor, precision=lax.Precision.HIGHEST)
    return (new_basis, rotated_moment)


def solution(mesh):
    placed = (P("row", "col"), P(("col", "row"), None), P(("col", "row"), None))
    return jax.shard_map(
        body,
        mesh=mesh,
        in_specs=placed,
        out_specs=(P(("col", "row"), None), P(("col", "row"), None)),
        check_vma=False,
    )
```

profile of v0, /device:TPU:1, one launch (start us, length us, event | category | flops | bytes accessed | tf_op | source)
XLA Modules:
  0.0 1323.2 jit_solution(17886480360487509458)
XLA Ops:
  12.8 72.0 %all-gather.2.cloned.1.call-done = bf16[1024,2048]{1,0:T(8,128)(2,1)} async-done(((bf16[128,2048]{1,0:T(8,128)(2,1)}), bf16[1024,2048]{1,0:T(8,128)(2,1)}) %all-gather.2.cloned.1.call-update) | async-done | bytes 4194320 | tf_op jit(solution)/shard_map/all_gather | solution.py:53
  84.8 15.1 %fusion.211 = f32[2048,2048]{1,0:T(8,128)} fusion(bf16[2048,1024]{1,0:T(8,128)(2,1)} %bitcast.219, bf16[1024,2048]{1,0:T(8,128)(2,1)} %all-gather.2.cloned.1.call-done), kind=kOutput, calls=%fused_computation.352 | convolution fusion | flops 8589934592 | bytes 25165824 | tf_op jit(solution)/shard_map/dot_general | solution.py:61
  99.9 178.9 %reduce-scatter.2.cloned.1.call-done = f32[128,2048]{1,0:T(8,128)} async-done(((f32[2048,2048]{1,0:T(8,128)}), f32[128,2048]{1,0:T(8,128)}) %reduce-scatter.2.cloned.1.call-update) | async-done | bytes 1048592 | tf_op jit(solution)/shard_map/reduce_scatter | solution.py:60
  280.2 15.1 %all_to_all.10 = bf16[8,2,8,2048]{3,2,1,0:T(8,128)(2,1)S(1)} all-to-all(bf16[8,2,8,2048]{3,2,1,0:T(8,128)(2,1)S(1)} %bitcast.220), channel_id=1, replica_groups=mesh['row'=8,'col'=16] {'row'}, dimensions={0} | all-to-all | bytes 1048576 | tf_op jit(solution)/shard_map/all_to_all | solution.py:67
  295.3 17.4 %all_to_all.11 = bf16[16,8,2048]{2,1,0:T(8,128)(2,1)S(1)} all-to-all(bf16[16,8,2048]{2,1,0:T(8,128)(2,1)S(1)} %bitcast.221), channel_id=1, replica_groups=mesh['row'=8,'col'=16] {'col'}, dimensions={0} | all-to-all | bytes 1048576 | tf_op jit(solution)/shard_map/all_to_all | solution.py:69
  322.1 211.6 %all-reduce.4.cloned.1.call-done = f32[2048,2048]{0,1:T(8,128)} async-done(((f32[2048,2048]{0,1:T(8,128)}), f32[2048,2048]{0,1:T(8,128)}) %all-reduce.4.cloned.1.call-update) | async-done | bytes 16777232 | tf_op jit(solution)/shard_map/psum | solution.py:75
  540.0 11.7 cholesky.462
  564.2 11.9 cholesky.481
  611.2 12.1 cholesky.519
  640.5 39.3 %custom-call.38 = f32[4,128,128]{1,2,0:T(8,128)S(1)} custom-call(f32[4,128,128]{2,1,0:T(8,128)S(1)} %get-tuple-element.30), custom_call_target="InvertDiagBlocksLowerTriangular" | custom-call | tf_op jit(solution)/shard_map/jit(_solve_triangular)/triangular_solve | solution.py:19
  686.7 12.4 fusion.27
  699.1 20.2 %slice_subtract_fusion = f32[1536,1536]{0,1:T(8,128)S(1)} fusion(f32[2048,2048]{0,1:T(8,128)} %all-reduce.4.cloned.1.call-done, f32[1536,512]{1,0:T(8,128)S(1)} %fusion.27), kind=kOutput, calls=%fused_computation.28 | convolution fusion | flops 14497873920 | bytes 25165824 | tf_op jit(solution)/shard_map/dot_general | solution.py:28
  779.4 13.2 cholesky.574
  836.6 39.3 %custom-call.42 = f32[4,128,128]{1,2,0:T(8,128)S(1)} custom-call(f32[4,128,128]{2,1,0:T(8,128)S(1)} %get-tuple-element.31), custom_call_target="InvertDiagBlocksLowerTriangular" | custom-call | tf_op jit(solution)/shard_map/jit(_solve_triangular)/triangular_solve | solution.py:19
  962.6 13.2 cholesky.646
  992.3 11.7 cholesky.663
  1011.4 13.6 %while.10 = (s32[]{:T(128)}, f32[512,512]{1,0:T(8,128)}, s32[4,2]{0,1:T(2,128)S(1)}, f32[4,128,128]{2,1,0:T(8,128)}, s32[]{:T(128)}) while((s32[]{:T(128)}, f32[512,512]{1,0:T(8,128)}, s32[4,2]{0,1:T(2,128)S(1)}, f32[4,128,128]{2,1,0:T(8,128)}, s32[]{:T(128)}) %tuple.126), condition=%wide.while_cond.clone.1, body=%wide.while_body.clone.1.sunk | while | flops 2 | bytes 132705 | solution.py:19
  1025.0 40.8 %custom-call.46 = f32[4,128,128]{1,2,0:T(8,128)} custom-call(f32[4,128,128]{2,1,0:T(8,128)} %get-tuple-element.32), custom_call_target="InvertDiagBlocksLowerTriangular" | custom-call | tf_op jit(solution)/shard_map/jit(_solve_triangular)/triangular_solve | solution.py:19
  1088.7 11.9 cholesky.678
  1147.4 13.4 %cholesky.718 = f32[128,128]{1,0:T(8,128)} custom-call(f32[128,128]{1,0:T(8,128)} %cholesky.794), custom_call_target="Cholesky" | custom-call | tf_op jit(solution)/shard_map/jit(cholesky)/cholesky | solution.py:18
  1177.4 11.7 cholesky.735
  1198.7 37.9 %fusion.29 = f32[128,2048]{0,1:T(8,128)} fusion(f32[128,2048]{1,0:T(8,128)S(1)} %copy-done, f32[512,512]{1,0:T(8,128)} %get-tuple-element.75, f32[512,512]{1,0:T(8,128)} %copy-done.8, f32[512,512]{1,0:T(8,128)} %get-tuple-element.77, f32[1024,512]{1,0:T(8,128)} %broadcast_in_dim.9, f32[1024,512]{1,0:T(8,128)S(1)} %fusion.35, ...), kind=kOutput, calls=%fused_computation.45 | convolution fusion | flops 6484393984 | bytes 15728640 | tf_op jit(solution)/shard_map/dot_general | solution.py:79
  1239.8 14.0 %while.11 = (s32[]{:T(128)}, f32[512,512]{1,0:T(8,128)}, s32[4,2]{0,1:T(2,128)S(1)}, f32[4,128,128]{2,1,0:T(8,128)}, s32[]{:T(128)}) while((s32[]{:T(128)}, f32[512,512]{1,0:T(8,128)}, s32[4,2]{0,1:T(2,128)S(1)}, f32[4,128,128]{2,1,0:T(8,128)}, s32[]{:T(128)}) %tuple.127), condition=%wide.while_cond.clone.2, body=%wide.while_body.clone.2.sunk | while | flops 2 | bytes 132705 | solution.py:19
  1253.9 40.9 %custom-call.50 = f32[4,128,128]{1,2,0:T(8,128)} custom-call(f32[4,128,128]{2,1,0:T(8,128)} %get-tuple-element.33), custom_call_target="InvertDiagBlocksLowerTriangular" | custom-call | tf_op jit(solution)/shard_map/jit(_solve_triangular)/triangular_solve | solution.py:19
  (313 shorter events, 469.1 us)
Async XLA Ops:
  7.2 1191.5 %copy-start = (f32[128,2048]{1,0:T(8,128)S(1)}, f32[128,2048]{1,0:T(8,128)}, u32[]{:S(2)}) copy-start(f32[128,2048]{1,0:T(8,128)} %param.8) | copy-start | bytes 3145732
  7.2 77.6 %all-gather.2.cloned.1.call-start = ((), (), s32[]{:S(2)}) async-start(), calls=%async_computation.3 | async-start | bytes 4718592 | tf_op jit(solution)/shard_map/all_gather | solution.py:53
  7.9 270.9 %reduce-scatter.2.cloned.1.call-start = ((), (), s32[]{:S(2)}) async-start(), calls=%async_computation.4 | async-start | bytes 17825792 | tf_op jit(solution)/shard_map/reduce_scatter | solution.py:60
  99.9 433.9 %all-reduce.4.cloned.1.call-start = ((), (), s32[]{:S(2)}) async-start(), calls=%async_computation.5 | async-start | bytes 33554432 | tf_op jit(solution)/shard_map/psum | solution.py:75
  312.7 8.2 copy-start.13
  320.9 559.0 %copy-start.5 = (f32[512,512]{1,0:T(8,128)}, f32[512,512]{1,0:T(8,128)S(1)}, u32[]{:S(2)}) copy-start(f32[512,512]{1,0:T(8,128)S(1)} %fusion.62) | copy-start | bytes 3145732
  681.9 17.2 %copy-start.19 = (f32[128,512]{1,0:T(8,128)}, f32[128,512]{1,0:T(8,128)S(1)}, u32[]{:S(2)}) copy-start(f32[128,512]{1,0:T(8,128)S(1)} %fusion.168) | copy-start | bytes 786436
  683.8 15.3 %copy-start.31 = (f32[128,512]{1,0:T(8,128)}, f32[128,512]{1,0:T(8,128)S(1)}, u32[]{:S(2)}) copy-start(f32[128,512]{1,0:T(8,128)S(1)} %fusion.166) | copy-start | bytes 786436
  686.7 12.4 copy-start.37
  699.1 20.2 %copy-start.1 = (f32[1536,512]{1,0:T(8,128)}, f32[1536,512]{1,0:T(8,128)S(1)}, u32[]{:S(2)}) copy-start(f32[1536,512]{1,0:T(8,128)S(1)} %fusion.27) | copy-start | bytes 9437188
  876.4 5.7 copy-start.15
  1065.8 10.2 copy-start.7
  1067.3 12.2 copy-start.17
  1070.1 9.5 copy-start.23
  1192.9 5.7 copy-start.2
  1294.8 5.8 copy-start.46
  1294.8 8.5 copy-start.20
  1294.8 8.5 copy-start.32
  1294.8 8.5 copy-start.38
  1297.6 7.5 copy-start.3
  1297.7 7.5 copy-start.26
  1301.0 5.3 copy-start.16
  1301.0 5.3 copy-start.22
  1301.0 5.3 copy-start.34
  (27 other events, 69.5 us)
Sparse Core Ops, SparseCore 0:
  10.4 74.3 all-gather.1
  100.0 178.8 reduce-scatter.1
  320.9 212.7 all-reduce.3
where the time goes:
time: 1330 us; the launch traced here: 1320 us
  other arithmetic  513 us (39%)
  waiting for transfers between devices  463 us (35%)
  matrix products  193 us (15%)
  local copies, waits for them, and re-layouts  95.1 us (7%)
  blocking collectives  32.5 us (2%)
  between operations  25.5 us (2%)
    another operation x59, other arithmetic, blocked_cholesky(): diag_factor = jnp.linalg.cholesky(head)  334 us
    psum x1, waiting for transfers between devices, body(): gram_matrix = lax.psum(gram_part, ('row', 'col'))  212 us
    reduce_scatter x1, waiting for transfers between devices, body(): lax.psum_scatter(jnp.dot(stripe, column_panel, preferred_element_type=jnp...  179 us
    another operation x9, other arithmetic, blocked_cholesky(): jax.scipy.linalg.solve_triangular(diag_factor, jnp.eye(step_width, dtype=...  169 us
    all_gather x1, waiting for transfers between devices, body(): column_panel = lax.all_gather(old_basis, 'row', axis=0, tiled=True)  72 us
    another operation x53, local copies, waits for them, and re-layouts, blocked_cholesky(): jax.scipy.linalg.solve_triangular(diag_factor, jnp.eye(step_width, dtype=...  52.1 us
    dot_general x1, matrix products, body(): jnp.dot(first_moment, lower_factor, precision=lax.Precision.HIGHEST)  37.9 us
    dot_general x3, matrix products, blocked_cholesky(): jnp.dot(below, below.T, precision=lax.Precision.HIGHEST)  32.2 us
  transfers between devices with their start and end apart: 3, of which 3 were waited for; matrix products, arithmetic and copies ran while one was open for 0% of the time, Pallas kernels for 0%

commit v1 on v0

v1 whole, which is shorter than its diff:
```python
import jax
import jax.numpy as jnp
from jax import lax
from jax.experimental import pallas as pl
from jax.experimental.pallas import tpu as pltpu
from jax.sharding import PartitionSpec as P

M = 16384
F32, BF = jnp.float32, jnp.bfloat16


def split(x):
    hi = x.astype(BF)
    return hi, (x - hi.astype(F32)).astype(BF)


def factor_block(d_ref, w_ref, width=16):
    n = 128
    rows_i = lax.broadcasted_iota(jnp.int32, (n, n), 0)
    cols_i = lax.broadcasted_iota(jnp.int32, (n, n), 1)
    w_ref[...] = jnp.where(rows_i == cols_i, 1.0, 0.0).astype(F32)
    np_ = n // width
    R, V = d_ref[:width, :], w_ref[:width, :]
    for p in range(np_):
        b0, m0, m1 = width * p, width * (p + 1), width * (p + 2)
        more = p < np_ - 1
        if more:
            N, NV = d_ref[m0:m1, :], w_ref[m0:m1, :]
            A = jnp.concatenate([R, N], 0)
            Z = jnp.concatenate([V, NV], 0)
        else:
            A, Z = R, V
        H = A.shape[0]
        C = [jnp.broadcast_to(A[:, b0 + b:b0 + b + 1], (H, n)) for b in range(width)]
        us, vs = [], []
        def sub(x, a):
            return x[a:a + 1, :]
        lo = 0
        for a in range(width):
            if a - lo == 8:
                C = [None if c is None else c[8:] for c in C]
                A, Z = A[8:], Z[8:]
                lo = a
            q = a - lo
            r = lax.rsqrt(sub(C[a], q))
            u, v = sub(A, q) * r, sub(Z, q) * r
            us.append(u); vs.append(v)
            ca = C[a] * r
            C[a] = None
            for b in range(a + 1, width):
                C[b] = C[b] - ca * jnp.broadcast_to(sub(ca, b - lo), ca.shape)
            A = A - ca * u
            Z = Z - ca * v
        U, W = jnp.concatenate(us, 0), jnp.concatenate(vs, 0)
        d_ref[b0:m0, :] = U
        w_ref[b0:m0, :] = W
        if more:
            R, V = A[width - lo:], Z[width - lo:]
        if p < np_ - 2:
            uh, ul = split(U)
            wh, wl = split(W)
            lhs = jnp.concatenate([uh, ul, uh], 0)
            rhs = jnp.concatenate([jnp.concatenate([uh, uh, ul], 0), jnp.concatenate([wh, wh, wl], 0)], 1)
            up = lax.dot_general(lhs, rhs, (((0,), (0,)), ((), ())), preferred_element_type=F32)
            d_ref[m1:, :] = d_ref[m1:, :] - up[m1:, :n]
            w_ref[m1:, :] = w_ref[m1:, :] - up[m1:, n:]
    d_ref[...] = jnp.where(rows_i <= cols_i, d_ref[...], 0.0)


B = 256
NT=(((1,),(1,)),((),()))
NN=(((1,),(0,)),((),()))
def mm(a,b,dims): return lax.dot_general(a,b,dims,preferred_element_type=F32)
def mm3(ah,al,bh,bl,dims): return mm(ah,bh,dims)+(mm(ah,bl,dims)+mm(al,bh,dims))
def mm3f(a,b,dims):
    ah,al=split(a); bh,bl=split(b)
    return mm3(ah,al,bh,bl,dims)

def factor_solve_kernel(g_ref, p_ref, m_ref, x_ref, y_ref, A, Lh, Ll, mh, ml, d_s, w_s, w_full, gsem):
    n = g_ref.shape[0]
    nb = n // B
    copies = [pltpu.make_async_copy(g_ref.at[pl.ds(k*B, n-k*B), pl.ds(k*B, B)], A.at[pl.ds(k*B, n-k*B), pl.ds(k*B, B)], gsem.at[k]) for k in range(nb)]
    for c in copies: c.start()
    A[n:n+128, :] = p_ref[...].astype(F32)
    A[n+128:, :] = jnp.zeros((128, n), F32)
    mhi, mlo = split(m_ref[...])
    mh[...] = mhi; ml[...] = mlo
    def blk(i, k): return (pl.ds(pl.multiple_of(i*B, B), B), pl.ds(pl.multiple_of(k*B, B), B))
    for c in copies: c.wait()
    def step(k, carry):
        def row_tile(i, _):
            t = blk(i, k)
            def inner(j, acc):
                a, b = blk(i, j), blk(k, j)
                return acc - mm3(Lh[a], Ll[a], Lh[b], Ll[b], NT)
            A[t] = lax.fori_loop(0, k, inner, A[t])
            return 0
        lax.fori_loop(k, nb+1, row_tile, 0)
        kk = pl.multiple_of(k*B, B)
        h = 128
        q0, q1 = pl.ds(kk, h), pl.ds(kk+h, h)
        d_s[...] = A[q0, q0]
        factor_block(d_s, w_s)
        w0 = w_s[...]
        l00 = d_s[...].T
        l10 = mm3f(A[q1, q0], w0, NT)
        d_s[...] = A[q1, q1] - mm3f(l10, l10, NT)
        factor_block(d_s, w_s)
        w1 = w_s[...]
        l11 = d_s[...].T
        w10 = -mm3f(w1, mm3f(l10, w0, NN), NN)
        w_full[:h, :h] = w0
        w_full[:h, h:] = jnp.zeros((h, h), F32)
        w_full[h:, :h] = w10
        w_full[h:, h:] = w1
        for (r, c, v) in ((q0,q0,l00),(q0,q1,jnp.zeros((h,h),F32)),(q1,q0,l10),(q1,q1,l11)):
            hi, lo = split(v)
            Lh[r,c]=hi; Ll[r,c]=lo
        wh, wl = split(w_full[...])
        def panel(i, _):
            t = blk(i, k)
            ah, al = split(A[t])
            v = mm3(ah, al, wh, wl, NT)
            hi, lo = split(v)
            Lh[t] = hi; Ll[t] = lo
            return 0
        lax.fori_loop(k+1, nb+1, panel, 0)
        x_ref[:, pl.ds(kk, B)] = (Lh[n:n+128, pl.ds(kk, B)].astype(F32)+Ll[n:n+128, pl.ds(kk, B)].astype(F32)).astype(BF)
        def yt(i, acc):
            a = pl.ds(pl.multiple_of(i*B,B),B)
            t = blk(i, k)
            return acc + mm3(mh[:, a], ml[:, a], Lh[t], Ll[t], NN)
        y_ref[:, pl.ds(kk, B)] = lax.fori_loop(k, nb, yt, jnp.zeros((128, B), F32))
        return carry
    lax.fori_loop(0, nb, step, 0)

def factor_solve(g, p, m):
    n=g.shape[0]
    return pl.pallas_call(factor_solve_kernel,
        out_shape=[jax.ShapeDtypeStruct((128,n),BF), jax.ShapeDtypeStruct((128,n),F32)],
        in_specs=[pl.BlockSpec(memory_space=pl.ANY), pl.BlockSpec(memory_space=pltpu.VMEM), pl.BlockSpec(memory_space=pltpu.VMEM)],
        out_specs=[pl.BlockSpec(memory_space=pltpu.VMEM)]*2,
        scratch_shapes=[pltpu.VMEM((n+B,n),F32),pltpu.VMEM((n+B,n),BF),pltpu.VMEM((n+B,n),BF),pltpu.VMEM((128,n),BF),pltpu.VMEM((128,n),BF),
          pltpu.VMEM((128,128),F32),pltpu.VMEM((128,128),F32),pltpu.VMEM((B,B),F32),pltpu.SemaphoreType.DMA((n//B,))],
        compiler_params=pltpu.CompilerParams(vmem_limit_bytes=60*2**20),
        name="factor_solve")(g,p,m)


def body(factor, old_basis, first_moment):
    grid_rows = lax.axis_size("row")
    grid_columns = lax.axis_size("col")
    tile_rows, tile_columns = factor.shape
    slab_rows, panel_width = old_basis.shape
    groups = grid_columns // grid_rows
    column_panel = lax.all_gather(old_basis, "row", axis=0, tiled=True)
    sub_rows = slab_rows // grid_columns
    arranged = factor.reshape(groups, grid_rows, grid_columns, sub_rows, tile_columns)
    stripe = arranged
    stripe = jnp.transpose(stripe, (2, 1, 0, 3, 4)).reshape(
        lax.axis_size("col") * slab_rows, tile_columns
    )
    summed = lax.psum_scatter(
        jnp.dot(stripe, column_panel, preferred_element_type=jnp.float32),
        "col",
        scatter_dimension=0,
        tiled=True,
    )
    relayed = summed.astype(jnp.bfloat16).reshape(grid_rows, groups, sub_rows, panel_width)
    relayed = lax.all_to_all(relayed, "row", split_axis=0, concat_axis=0, tiled=True)
    relayed = relayed.reshape(grid_columns, sub_rows, panel_width)
    relayed = lax.all_to_all(relayed, "col", split_axis=0, concat_axis=0, tiled=True)
    product = relayed.reshape(slab_rows, panel_width)
    gram_part = lax.dot_general(
        product, product, (((0,), (0,)), ((), ())), preferred_element_type=jnp.float32
    )
    gram_part = gram_part * (1.0 / M)
    gram_matrix = lax.psum(gram_part, ("row", "col"))
    new_basis, rotated_moment = factor_solve(gram_matrix, product, first_moment)
    return (new_basis, rotated_moment)


def solution(mesh):
    placed = (P("row", "col"), P(("col", "row"), None), P(("col", "row"), None))
    return jax.shard_map(
        body,
        mesh=mesh,
        in_specs=placed,
        out_specs=(P(("col", "row"), None), P(("col", "row"), None)),
        check_vma=False,
    )
```

time: 1330 us -> 652 us (0.49)
  other arithmetic: 513 us -> 1.28 us
  matrix products: 193 us -> 23.3 us
  Pallas kernels: 0 us -> 111 us
  local copies, waits for them, and re-layouts: 95.1 us -> 4.8 us
    another operation x68 -> x0, other arithmetic: 504 us -> none  [the longest x59 334 us: blocked_cholesky(): diag_factor = jnp.linalg.cholesky(head)]
    pallas_call x0 -> x1, Pallas kernels: none -> 111 us  [factor_solve(): pl.pallas_call(factor_solve_kernel, out_shape=[jax.ShapeDtypeStruct((128,...]
    dot_general x14 -> x0, matrix products: 106 us -> none  [the longest x1 37.9 us: body(): jnp.dot(first_moment, lower_factor, precision=lax.Precision.HIGHEST)]
    another operation x52 -> x0, matrix products: 63.3 us -> none  [the longest x24 32.2 us: blocked_cholesky(): diag_factor = jnp.linalg.cholesky(head)]
    another operation x72 -> x0, local copies, waits for them, and re-layouts: 61.1 us -> none  [the longest x53 52.1 us: blocked_cholesky(): jax.scipy.linalg.solve_triangular(diag_factor, jnp.eye(step_width, dtype=...]
    unnamed x97 -> x2, local copies, waits for them, and re-layouts: 15.1 us -> 0.01 us
  transfers between devices with their start and end apart: 3 -> 3, of which waited for: 3 -> 3; matrix products, arithmetic and copies ran while one was open for 0% -> 1% of each run, Pallas kernels for 0% -> 0%
where the time goes in v1:
time: 652 us
  waiting for transfers between devices  465 us (71%)
  Pallas kernels  111 us (17%)
  blocking collectives  32.5 us (5%)
  matrix products  23.3 us (4%)
  between operations  13.8 us (2%)
    psum x1, waiting for transfers between devices, body(): gram_matrix = lax.psum(gram_part, ('row', 'col'))  213 us
    reduce_scatter x1, waiting for transfers between devices, body(): lax.psum_scatter(jnp.dot(stripe, column_panel, preferred_element_type=jnp...  179 us
    pallas_call x1, Pallas kernels, factor_solve(): pl.pallas_call(factor_solve_kernel, out_shape=[jax.ShapeDtypeStruct((128,...  111 us
    all_gather x1, waiting for transfers between devices, body(): column_panel = lax.all_gather(old_basis, 'row', axis=0, tiled=True)  72 us
    all_to_all x1, blocking collectives, body(): lax.all_to_all(relayed, 'col', split_axis=0, concat_axis=0, tiled=True)  17.4 us
    dot_general x1, matrix products, body(): jnp.dot(stripe, column_panel, preferred_element_type=jnp.float32)  15.2 us
    all_to_all x1, blocking collectives, body(): lax.all_to_all(relayed, 'row', split_axis=0, concat_axis=0, tiled=True)  15.1 us
  transfers between devices with their start and end apart: 3, of which 3 were waited for; matrix products, arithmetic and copies ran while one was open for 1% of the time, Pallas kernels for 0%

profile of v1, /device:TPU:1, one launch (start us, length us, event | category | flops | bytes accessed | tf_op | source)
XLA Modules:
  0.0 651.6 jit_solution(842477722575741971)
XLA Ops:
  7.2 0.0 all-gather.2.cloned.1.call-start
  7.2 0.7 all-gather.2.cloned.1.call-update
  7.9 0.0 reduce-scatter.2.cloned.1.call-start
  7.9 4.8 copy.12
  12.7 72.0 %all-gather.2.cloned.1.call-done = bf16[1024,2048]{1,0:T(8,128)(2,1)} async-done(((bf16[128,2048]{1,0:T(8,128)(2,1)}), bf16[1024,2048]{1,0:T(8,128)(2,1)}) %all-gather.2.cloned.1.call-update) | async-done | bytes 4194320 | tf_op jit(solution)/shard_map/all_gather | solution.py:155
  84.8 15.2 %fusion = f32[2048,2048]{1,0:T(8,128)} fusion(bf16[2048,1024]{1,0:T(8,128)(2,1)} %bitcast.14, bf16[1024,2048]{1,0:T(8,128)(2,1)} %all-gather.2.cloned.1.call-done), kind=kOutput, calls=%fused_computation.1 | convolution fusion | flops 8589934592 | bytes 25165824 | tf_op jit(solution)/shard_map/dot_general | solution.py:163
  100.0 0.0 reduce-scatter.2.cloned.1.call-update
  100.0 0.0 all-reduce.2.cloned.1.call-start
  100.0 178.9 %reduce-scatter.2.cloned.1.call-done = f32[128,2048]{1,0:T(8,128)} async-done(((f32[2048,2048]{1,0:T(8,128)}), f32[128,2048]{1,0:T(8,128)}) %reduce-scatter.2.cloned.1.call-update) | async-done | bytes 1048592 | tf_op jit(solution)/shard_map/reduce_scatter | solution.py:162
  278.9 1.3 convert_element_type.3
  280.2 15.1 %all_to_all.10 = bf16[8,2,8,2048]{3,2,1,0:T(8,128)(2,1)S(1)} all-to-all(bf16[8,2,8,2048]{3,2,1,0:T(8,128)(2,1)S(1)} %bitcast.16), channel_id=1, replica_groups=mesh['row'=8,'col'=16] {'row'}, dimensions={0} | all-to-all | bytes 1048576 | tf_op jit(solution)/shard_map/all_to_all | solution.py:169
  295.4 17.4 %all_to_all.11 = bf16[16,8,2048]{2,1,0:T(8,128)(2,1)S(1)} all-to-all(bf16[16,8,2048]{2,1,0:T(8,128)(2,1)S(1)} %bitcast.17), channel_id=1, replica_groups=mesh['row'=8,'col'=16] {'col'}, dimensions={0} | all-to-all | bytes 1048576 | tf_op jit(solution)/shard_map/all_to_all | solution.py:171
  312.8 0.0 copy-start
  312.8 8.1 %bitcast_multiply_fusion = f32[2048,2048]{1,0:T(8,128)} fusion(bf16[16,8,2048]{2,1,0:T(8,128)(2,1)S(1)} %all_to_all.11), kind=kOutput, calls=%fused_computation | convolution fusion | flops 1077936128 | bytes 17301504 | tf_op jit(solution)/shard_map/dot_general | solution.py:173
  320.9 0.0 copy-done
  320.9 0.0 all-reduce.2.cloned.1.call-update
  320.9 213.1 %all-reduce.2.cloned.1.call-done.g_ref = f32[2048,2048]{1,0:T(8,128)} async-done(((f32[2048,2048]{1,0:T(8,128)}), f32[2048,2048]{1,0:T(8,128)}) %all-reduce.2.cloned.1.call-update) | async-done | bytes 16777232 | tf_op jit(solution)/shard_map/psum | solution.py:177
  534.0 111.0 %factor_solve.1 = (bf16[128,2048]{1,0:T(8,128)(2,1)}, f32[128,2048]{1,0:T(8,128)}) custom-call(f32[2048,2048]{1,0:T(8,128)} %all-reduce.2.cloned.1.call-done.g_ref, bf16[128,2048]{1,0:T(8,128)(2,1)} %bitcast.15, f32[128,2048]{1,0:T(8,128)} %m_ref.1), custom_call_target="tpu_custom_call" | custom-call | tf_op jit(solution)/shard_map/factor_solve/pallas_call | solution.py:139
Async XLA Ops:
  7.2 77.6 %all-gather.2.cloned.1.call-start = ((), (), s32[]{:S(2)}) async-start(), calls=%async_computation.3 | async-start | bytes 4718592 | tf_op jit(solution)/shard_map/all_gather | solution.py:155
  7.9 271.1 %reduce-scatter.2.cloned.1.call-start = ((), (), s32[]{:S(2)}) async-start(), calls=%async_computation.4 | async-start | bytes 17825792 | tf_op jit(solution)/shard_map/reduce_scatter | solution.py:162
  100.0 434.0 %all-reduce.2.cloned.1.call-start = ((), (), s32[]{:S(2)}) async-start(), calls=%async_computation.5 | async-start | bytes 33554432 | tf_op jit(solution)/shard_map/psum | solution.py:177
  312.8 8.1 %copy-start = (bf16[16,8,2048]{2,1,0:T(8,128)(2,1)}, bf16[16,8,2048]{2,1,0:T(8,128)(2,1)S(1)}, u32[]{:S(2)}) copy-start(bf16[16,8,2048]{2,1,0:T(8,128)(2,1)S(1)} %all_to_all.11) | copy-start | bytes 1572868
Sparse Core Ops, SparseCore 0:
  10.3 74.3 all-gather.1
  100.1 178.8 reduce-scatter.1
  321.0 212.9 all-reduce.1

commit v2 on v1

--- a/solution.py
+++ b/solution.py
@@ -1,3 +1,5 @@
+import functools
+
 import jax
 import jax.numpy as jnp
 from jax import lax
@@ -7,6 +9,262 @@
 
 M = 16384
 F32, BF = jnp.float32, jnp.bfloat16
+MESH = pl.DeviceIdType.MESH
+TN = (((0,), (0,)), ((), ()))
+
+def coords():
+    row, col = lax.axis_index("row"), lax.axis_index("col")
+    return (row % 2) * 2 + (col // 2) % 2, col // 4, row // 2, col % 2
+
+def device(x, y, z, core):
+    return (z * 2 + x // 2, y * 4 + (x % 2) * 2 + core)
+
+def links(x, y, z, core):
+    near = lambda v: v + 1 - 2 * (v % 2)
+    far = lambda v: 3 - v
+    low = lambda v: (v + v // 2) % 2
+    peers = [device(near(x), y, z, core), device(x, near(y), z, core), device(x, y, near(z), core),
+             device(far(x), y, z, core), device(x, far(y), z, core), device(x, y, far(z), core)]
+    bits = [low(x), low(y), low(z), x // 2, y // 2, z // 2]
+    return peers, bits
+
+def strips(n):
+    lens = [n // 256 - c // 2 for c in range(n // 128)]
+    starts = [sum(lens[:c]) for c in range(len(lens) + 1)]
+    return lens, starts
+
+def remote(src, dst, ssem, rsem, dev):
+    return pltpu.make_async_remote_copy(src, dst, ssem, rsem, device_id=dev, device_id_type=MESH)
+
+def gram_kernel(p_ref, g_ref, own_ref, W, RB, O, ss, rs, as_, ar, fs, fr, ls, ps, pr):
+    x, y, z, core = coords()
+    row, col = lax.axis_index("row"), lax.axis_index("col")
+    peers, bits = links(x, y, z, core)
+    sib = device(x, y, z, 1 - core)
+    n = p_ref.shape[1]
+    lens, starts = strips(n)
+    parts, rows = W.shape[0], W.shape[1]
+    tiles = rows // 256
+    j = 2 * (col // 2) + 1 - core
+    to = (j % 8, 2 * row + j // 8)
+    i = (col % 2) * 8 + row
+    frm = (col // 2, (i // 2) * 2 + 1 - i % 2)
+    bar = pltpu.get_barrier_semaphore()
+    for d in peers + [sib, frm]:
+        pl.semaphore_signal(bar, inc=1, device_id=d, device_id_type=MESH)
+    pl.semaphore_wait(bar, 8)
+
+    def tile(s, u, _):
+        U = core * (parts * tiles) + s * tiles + u
+        c, st = 0, 0
+        for q in range(1, len(lens)):
+            past = (U >= starts[q]).astype(jnp.int32)
+            c, st = c + past, st + past * lens[q - 1]
+        i = U - st + c // 2
+        a = p_ref[:, pl.ds(pl.multiple_of(i * 256, 256), 256)]
+        b = p_ref[:, pl.ds(pl.multiple_of(c * 128, 128), 128)]
+        W[s, pl.ds(pl.multiple_of(u * 256, 256), 256), :] = lax.dot_general(a, b, TN, preferred_element_type=F32) * (1.0 / M)
+        return 0
+
+    slab = remote(p_ref.at[pl.ds(pl.multiple_of((1 - core) * 128, 128), 128), :], own_ref, ps, pr, to)
+    slab.start()
+
+    off = [0] * parts
+    steps = len(peers)
+    sends = []
+    def send(t, s):
+        h = rows >> (t + 1)
+        d = (s + t) % steps
+        src = W.at[s, pl.ds(pl.multiple_of(off[s] + (1 - bits[d]) * h, 8), h), :]
+        c = remote(src, RB.at[s, pl.ds(rows - 2 * h, h), :], ss.at[t, s], rs.at[t, s], peers[d])
+        c.start()
+        return c
+    cur = []
+    for s in range(parts):
+        lax.fori_loop(0, tiles, functools.partial(tile, s), 0)
+        cur.append(send(0, s))
+    for t in range(steps):
+        h = rows >> (t + 1)
+        nxt = []
+        for s in range(parts):
+            cur[s].wait_recv()
+            d = (s + t) % steps
+            off[s] = off[s] + bits[d] * h
+            at = pl.ds(pl.multiple_of(off[s], 8), h)
+            if t < steps - 1:
+                W[s, at, :] = W[s, at, :] + RB[s, pl.ds(rows - 2 * h, h), :]
+                sends.append(cur[s])
+                nxt.append(send(t + 1, s))
+            else:
+                O[s, at, :] = W[s, at, :] + RB[s, pl.ds(rows - 2 * h, h), :]
+                sends.append(cur[s])
+        cur = nxt
+    tail = []
+    def share(s, at, q):
+        c = remote(O.at[s, at, :], g_ref.at[core, s, at, :], fs.at[q, s], fr.at[q, s], sib)
+        l = pltpu.make_async_copy(O.at[s, at, :], g_ref.at[core, s, at, :], ls.at[q, s])
+        c.start(); l.start()
+        tail.append((c, l))
+    def give(t, s):
+        h = rows >> (t + 1)
+        at = pl.ds(pl.multiple_of(off[s], 8), h)
+        c = remote(O.at[s, at, :], O.at[s, at, :], as_.at[t, s], ar.at[t, s], peers[(s + t) % steps])
+        c.start()
+        return c
+    cur = [give(steps - 1, s) for s in range(parts)]
+    for t in range(steps - 1, -1, -1):
+        h = rows >> (t + 1)
+        nxt = []
+        for s in range(parts):
+            cur[s].wait_recv()
+            b = bits[(s + t) % steps]
+            got = off[s] + (1 - 2 * b) * h
+            off[s] = off[s] - b * h
+            sends.append(cur[s])
+            if t > 0:
+                nxt.append(give(t - 1, s))
+            if t == 2:
+                share(s, pl.ds(pl.multiple_of(off[s], 8), 2 * h), 2)
+            elif t < 2:
+                share(s, pl.ds(pl.multiple_of(got, 8), h), t)
+        cur = nxt
+    for c in sends:
+        c.wait_send()
+    for c, l in tail:
+        l.wait()
+        c.wait()
+    slab.wait()
+
+def gram_sum(p2):
+    n = p2.shape[1]
+    lens, starts = strips(n)
+    rows = starts[-1] * 256 // 12
+    dma = pltpu.SemaphoreType.DMA
+    return pl.pallas_call(
+        gram_kernel,
+        out_shape=[jax.ShapeDtypeStruct((2, 6, rows, 128), F32), jax.ShapeDtypeStruct((128, n), BF)],
+        in_specs=[pl.BlockSpec(memory_space=pltpu.VMEM)],
+        out_specs=[pl.BlockSpec(memory_space=pl.ANY)] * 2,
+        scratch_shapes=[pltpu.VMEM((6, rows, 128), F32)] * 3 + [dma((6, 6))] * 4 + [dma((3, 6))] * 3 + [dma(())] * 2,
+        compiler_params=pltpu.CompilerParams(collective_id=1, has_side_effects=True, vmem_limit_bytes=40 * 2**20),
+        name="gram_sum",
+    )(p2)
+
+
+NN = (((1,), (0,)), ((), ()))
+
+def product_kernel(f_ref, q_ref, p_ref, F, Q, S, own, YR, XS, XR, P2, fsem, qs, qr, gs, gr, ys, yr, xs, xr, ps, pr):
+    x, y, z, core = coords()
+    row, col = lax.axis_index("row"), lax.axis_index("col")
+    chunks, wide = Q.shape[0], Q.shape[3]
+    half = chunks * wide
+    sib = device(x, y, z, 1 - core)
+    across = device((x + 2) % 4, y, z, core)
+    beside = device(x + 1 - 2 * (x % 2), y, z, core)
+    zs = [device(x, y, (z + k) % 4, core) for k in (1, 2, 3)]
+    yy = [device(x, (y + k) % 4, z, core) for k in (1, 2, 3)]
+    bar = pltpu.get_barrier_semaphore()
+    for d in [sib, across, beside] + zs + yy:
+        pl.semaphore_signal(bar, inc=1, device_id=d, device_id_type=MESH)
+    pl.semaphore_wait(bar, 9)
+    lane = lambda first: pl.ds(pl.multiple_of(first, 128), wide)
+    mine = pl.ds(pl.multiple_of(row * 128, 128), 128)
+    acro = pl.ds(pl.multiple_of((row + 1 - 2 * (row % 2)) * 128, 128), 128)
+    sends = []
+    def go(c):
+        c.start()
+        sends.append(c)
+        return c
+    sq = [go(remote(q_ref.at[:, lane((1 - core) * half + ch * wide)], Q.at[ch, 1, mine, :], qs.at[ch], qr.at[ch], sib)) for ch in range(chunks)]
+    fr = go(remote(f_ref, F.at[1], fsem.at[0], fsem.at[1], sib))
+    fl = pltpu.make_async_copy(f_ref, F.at[0], fsem.at[2])
+    fl.start()
+    for ch in range(chunks):
+        Q[ch, 0, mine, :] = q_ref[:, lane(core * half + ch * wide)]
+    def gat(ch, i, at, d):
+        return go(remote(Q.at[ch, :, at, :], Q.at[ch, :, at, :], gs.at[ch, i], gr.at[ch, i], d))
+    gx, gz = [], [[] for _ in range(chunks)]
+    for ch in range(chunks):
+        sq[ch].wait_recv()
+        gx.append(gat(ch, 0, mine, across))
+    def near(ch):
+        for k in range(3):
+            gz[ch].append(gat(ch, 1 + k, mine, zs[k]))
+    def forward(ch):
+        gx[ch].wait_recv()
+        for k in range(3):
+            gz[ch].append(gat(ch, 4 + k, acro, zs[k]))
+    near(0)
+    forward(0)
+    ysend = [[] for _ in range(chunks)]
+    xsend, psend = [None] * chunks, [None] * chunks
+    xl = x % 2
+    keep = pl.ds(pl.multiple_of(xl * 256, 256), 256)
+    give = pl.ds(pl.multiple_of((1 - xl) * 256, 256), 256)
+    def multiply(ch):
+        for k in (2, 1, 3, 0):
+            at = pl.ds(pl.multiple_of(((y + k) % 4) * 512, 512), 512)
+            v = lax.dot_general(F[0, at, :], Q[ch, 0], NN, preferred_element_type=F32)
+            v = v + lax.dot_general(F[1, at, :], Q[ch, 1], NN, preferred_element_type=F32)
+            if k == 0:
+                own[ch] = v
+            else:
+                S[ch, k - 1] = v.astype(BF)
+                ysend[ch].append(go(remote(S.at[ch, k - 1], YR.at[ch, k - 1], ys.at[ch, k - 1], yr.at[ch, k - 1], yy[k - 1])))
+    def add(ch):
+        for c in ysend[ch]:
+            c.wait_recv()
+        def total(at):
+            return own[ch, at, :] + ((YR[ch, 0, at, :].astype(F32) + YR[ch, 1, at, :].astype(F32)) + YR[ch, 2, at, :].astype(F32))
+        XS[ch] = total(give)
+        xsend[ch] = go(remote(XS.at[ch], XR.at[ch], xs.at[ch], xr.at[ch], beside))
+        own[ch, keep, :] = total(keep)
+    def finish(ch):
+        xsend[ch].wait_recv()
+        at = lane(core * half + ch * wide)
+        P2[:, at] = (own[ch, keep, :] + XR[ch]).astype(BF)
+        psend[ch] = go(remote(P2.at[:, at], P2.at[:, at], ps.at[ch], pr.at[ch], sib))
+    for ch in range(chunks):
+        if ch + 1 < chunks:
+            near(ch + 1)
+            forward(ch + 1)
+        for c in gz[ch]:
+            c.wait_recv()
+        if ch == 0:
+            fl.wait()
+            fr.wait_recv()
+        multiply(ch)
+        if ch >= 1:
+            add(ch - 1)
+        if ch >= 2:
+            finish(ch - 2)
+    add(chunks - 1)
+    finish(chunks - 2)
+    finish(chunks - 1)
+    for c in psend:
+        c.wait_recv()
+    p_ref[...] = P2[...]
+    for c in sends:
+        c.wait_send()
+
+def product_rows(factor, slab, chunks=4):
+    n = slab.shape[1]
+    rows, cols = factor.shape
+    wide = n // 2 // chunks
+    dma = pltpu.SemaphoreType.DMA
+    vm = pltpu.VMEM
+    return pl.pallas_call(
+        product_kernel,
+        out_shape=jax.ShapeDtypeStruct((256, n), BF),
+        in_specs=[pl.BlockSpec(memory_space=pl.ANY), pl.BlockSpec(memory_space=pltpu.VMEM)],
+        out_specs=pl.BlockSpec(memory_space=pltpu.VMEM),
+        scratch_shapes=[vm((2, rows, cols), BF), vm((chunks, 2, cols, wide), BF), vm((chunks, 3, 512, wide), BF),
+            vm((chunks, 512, wide), F32), vm((chunks, 3, 512, wide), BF), vm((chunks, 256, wide), F32), vm((chunks, 256, wide), F32),
+            vm((256, n), BF), dma((3,)), dma((chunks,)), dma((chunks,)), dma((chunks, 7)), dma((chunks, 7)),
+            dma((chunks, 3)), dma((chunks, 3)), dma((chunks,)), dma((chunks,)), dma((chunks,)), dma((chunks,))],
+        compiler_params=pltpu.CompilerParams(collective_id=0, has_side_effects=True, vmem_limit_bytes=48 * 2**20),
+        name="product_rows",
+    )(factor, slab)
 
 
 def split(x):
@@ -77,9 +335,17 @@
     return mm3(ah,al,bh,bl,dims)
 
 def factor_solve_kernel(g_ref, p_ref, m_ref, x_ref, y_ref, A, Lh, Ll, mh, ml, d_s, w_s, w_full, gsem):
-    n = g_ref.shape[0]
+    n = p_ref.shape[1]
     nb = n // B
-    copies = [pltpu.make_async_copy(g_ref.at[pl.ds(k*B, n-k*B), pl.ds(k*B, B)], A.at[pl.ds(k*B, n-k*B), pl.ds(k*B, B)], gsem.at[k]) for k in range(nb)]
+    lens, starts = strips(n)
+    copies = [
+        pltpu.make_async_copy(
+            g_ref.at[pl.ds(starts[c] * B, lens[c] * B), :],
+            A.at[pl.ds((c // 2) * B, lens[c] * B), pl.ds(c * 128, 128)],
+            gsem.at[c],
+        )
+        for c in range(len(lens))
+    ]
     for c in copies: c.start()
     A[n:n+128, :] = p_ref[...].astype(F32)
     A[n+128:, :] = jnp.zeros((128, n), F32)
@@ -135,47 +401,21 @@
     lax.fori_loop(0, nb, step, 0)
 
 def factor_solve(g, p, m):
-    n=g.shape[0]
+    n = p.shape[1]
     return pl.pallas_call(factor_solve_kernel,
         out_shape=[jax.ShapeDtypeStruct((128,n),BF), jax.ShapeDtypeStruct((128,n),F32)],
         in_specs=[pl.BlockSpec(memory_space=pl.ANY), pl.BlockSpec(memory_space=pltpu.VMEM), pl.BlockSpec(memory_space=pltpu.VMEM)],
         out_specs=[pl.BlockSpec(memory_space=pltpu.VMEM)]*2,
         scratch_shapes=[pltpu.VMEM((n+B,n),F32),pltpu.VMEM((n+B,n),BF),pltpu.VMEM((n+B,n),BF),pltpu.VMEM((128,n),BF),pltpu.VMEM((128,n),BF),
-          pltpu.VMEM((128,128),F32),pltpu.VMEM((128,128),F32),pltpu.VMEM((B,B),F32),pltpu.SemaphoreType.DMA((n//B,))],
+          pltpu.VMEM((128,128),F32),pltpu.VMEM((128,128),F32),pltpu.VMEM((B,B),F32),pltpu.SemaphoreType.DMA((n//128,))],
         compiler_params=pltpu.CompilerParams(vmem_limit_bytes=60*2**20),
         name="factor_solve")(g,p,m)
 
 
 def body(factor, old_basis, first_moment):
-    grid_rows = lax.axis_size("row")
-    grid_columns = lax.axis_size("col")
-    tile_rows, tile_columns = factor.shape
-    slab_rows, panel_width = old_basis.shape
-    groups = grid_columns // grid_rows
-    column_panel = lax.all_gather(old_basis, "row", axis=0, tiled=True)
-    sub_rows = slab_rows // grid_columns
-    arranged = factor.reshape(groups, grid_rows, grid_columns, sub_rows, tile_columns)
-    stripe = arranged
-    stripe = jnp.transpose(stripe, (2, 1, 0, 3, 4)).reshape(
-        lax.axis_size("col") * slab_rows, tile_columns
-    )
-    summed = lax.psum_scatter(
-        jnp.dot(stripe, column_panel, preferred_element_type=jnp.float32),
-        "col",
-        scatter_dimension=0,
-        tiled=True,
-    )
-    relayed = summed.astype(jnp.bfloat16).reshape(grid_rows, groups, sub_rows, panel_width)
-    relayed = lax.all_to_all(relayed, "row", split_axis=0, concat_axis=0, tiled=True)
-    relayed = relayed.reshape(grid_columns, sub_rows, panel_width)
-    relayed = lax.all_to_all(relayed, "col", split_axis=0, concat_axis=0, tiled=True)
-    product = relayed.reshape(slab_rows, panel_width)
-    gram_part = lax.dot_general(
-        product, product, (((0,), (0,)), ((), ())), preferred_element_type=jnp.float32
-    )
-    gram_part = gram_part * (1.0 / M)
-    gram_matrix = lax.psum(gram_part, ("row", "col"))
-    new_basis, rotated_moment = factor_solve(gram_matrix, product, first_moment)
+    rows = product_rows(factor, old_basis)
+    gram, product = gram_sum(rows)
+    new_basis, rotated_moment = factor_solve(gram.reshape(-1, 128), product, first_moment)
     return (new_basis, rotated_moment)
 
 

time: 652 us -> 293 us (0.45)
  waiting for transfers between devices: 465 us -> 0 us
  Pallas kernels: 111 us -> 284 us
  blocking collectives: 32.5 us -> 0 us
  matrix products: 23.3 us -> 0 us
  between operations: 13.8 us -> 0.82 us
    psum x1 -> x0, waiting for transfers between devices: 213 us -> none  [body(): gram_matrix = lax.psum(gram_part, ('row', 'col'))]
    reduce_scatter x1 -> x0, waiting for transfers between devices: 179 us -> none  [body(): lax.psum_scatter(jnp.dot(stripe, column_panel, preferred_element_type=jnp...]
    pallas_call x0 -> x2, Pallas kernels: none -> 173 us  [the longest x1 91.9 us: gram_sum(): pl.pallas_call(gram_kernel, out_shape=[jax.ShapeDtypeStruct((2, 6, rows,...]
    all_gather x1 -> x0, waiting for transfers between devices: 72 us -> none  [body(): column_panel = lax.all_gather(old_basis, 'row', axis=0, tiled=True)]
    all_to_all x2 -> x0, blocking collectives: 32.5 us -> none  [the longest x1 17.4 us: body(): lax.all_to_all(relayed, 'col', split_axis=0, concat_axis=0, tiled=True)]
    dot_general x2 -> x0, matrix products: 23.3 us -> none  [the longest x1 15.2 us: body(): jnp.dot(stripe, column_panel, preferred_element_type=jnp.float32)]
    unnamed x2 -> x8, local copies, waits for them, and re-layouts: 0.01 us -> 7.62 us
  transfers between devices with their start and end apart: 3 -> 0, of which waited for: 3 -> 0; matrix products, arithmetic and copies ran while one was open for 1% -> 0% of each run, Pallas kernels for 0% -> 0%
where the time goes in v2:
time: 293 us
  Pallas kernels  284 us (97%)
  local copies, waits for them, and re-layouts  7.62 us (3%)
    pallas_call x1, Pallas kernels, factor_solve(): pl.pallas_call(factor_solve_kernel, out_shape=[jax.ShapeDtypeStruct((128,...  111 us
    pallas_call x1, Pallas kernels, gram_sum(): pl.pallas_call(gram_kernel, out_shape=[jax.ShapeDtypeStruct((2, 6, rows,...  91.9 us
    pallas_call x1, Pallas kernels, product_rows(): pl.pallas_call(product_kernel, out_shape=jax.ShapeDtypeStruct((256, n), B...  81.4 us
    unnamed x8, local copies, waits for them, and re-layouts  7.62 us

profile of v2, /device:TPU:1, one launch (start us, length us, event | category | flops | bytes accessed | tf_op | source)
XLA Modules:
  0.0 292.8 jit_solution(2731789049922048442)
XLA Ops:
  0.6 0.0 copy-start.1
  0.6 2.2 copy-done.1
  2.8 0.0 copy-start.2
  2.8 1.0 copy-done.2
  3.9 81.4 %product_rows.1.p_ref = bf16[256,2048]{1,0:T(8,128)(2,1)S(1)} custom-call(bf16[2048,1024]{1,0:T(8,128)(2,1)S(1)} %copy-done.1, bf16[128,2048]{1,0:T(8,128)(2,1)S(1)} %copy-done.2), custom_call_target="tpu_custom_call" | custom-call | tf_op jit(solution)/shard_map/product_rows/pallas_call | solution.py:256
  85.3 91.9 %gram_sum.1 = (f32[2,6,1536,128]{3,2,1,0:T(8,128)S(1)}, bf16[128,2048]{1,0:T(8,128)(2,1)S(1)}) custom-call(bf16[256,2048]{1,0:T(8,128)(2,1)S(1)} %product_rows.1.p_ref), custom_call_target="tpu_custom_call" | custom-call | tf_op jit(solution)/shard_map/gram_sum/pallas_call | solution.py:143
  177.2 0.0 copy-start
  177.2 3.6 %copy-done = f32[2,6,1536,128]{3,2,1,0:T(8,128)} copy-done((f32[2,6,1536,128]{3,2,1,0:T(8,128)}, f32[2,6,1536,128]{3,2,1,0:T(8,128)S(1)}, u32[]{:S(2)}) %copy-start) | copy-done | bytes 9437208
  180.8 0.0 copy-start.3
  180.8 0.8 copy-done.3
  181.6 111.1 %factor_solve.1 = (bf16[128,2048]{1,0:T(8,128)(2,1)}, f32[128,2048]{1,0:T(8,128)}) custom-call(f32[18432,128]{1,0:T(8,128)} %bitcast.1, bf16[128,2048]{1,0:T(8,128)(2,1)} %copy-done.3, f32[128,2048]{1,0:T(8,128)} %m_ref.1), custom_call_target="tpu_custom_call" | custom-call | tf_op jit(solution)/shard_map/factor_solve/pallas_call | solution.py:405
Async XLA Ops:
  0.6 2.2 copy-start.1
  2.8 1.0 copy-start.2
  177.2 3.6 %copy-start = (f32[2,6,1536,128]{3,2,1,0:T(8,128)}, f32[2,6,1536,128]{3,2,1,0:T(8,128)S(1)}, u32[]{:S(2)}) copy-start(f32[2,6,1536,128]{3,2,1,0:T(8,128)S(1)} %get-tuple-element.4) | copy-start | bytes 28311556
  180.8 0.8 copy-start.3

commit v3 on v2

--- a/solution.py
+++ b/solution.py
@@ -150,8 +150,6 @@
         name="gram_sum",
     )(p2)
 
-
-NN = (((1,), (0,)), ((), ()))
 
 def product_kernel(f_ref, q_ref, p_ref, F, Q, S, own, YR, XS, XR, P2, fsem, qs, qr, gs, gr, ys, yr, xs, xr, ps, pr):
     x, y, z, core = coords()
@@ -272,7 +270,7 @@
     return hi, (x - hi.astype(F32)).astype(BF)
 
 
-def factor_block(d_ref, w_ref, width=16):
+def factor_block(d_ref, w_ref, slot, width=16):
     n = 128
     rows_i = lax.broadcasted_iota(jnp.int32, (n, n), 0)
     cols_i = lax.broadcasted_iota(jnp.int32, (n, n), 1)
@@ -289,6 +287,7 @@
         else:
             A, Z = R, V
         H = A.shape[0]
+        fin = slot(p)
         C = [jnp.broadcast_to(A[:, b0 + b:b0 + b + 1], (H, n)) for b in range(width)]
         us, vs = [], []
         def sub(x, a):
@@ -314,6 +313,7 @@
         w_ref[b0:m0, :] = W
         if more:
             R, V = A[width - lo:], Z[width - lo:]
+        fin()
         if p < np_ - 2:
             uh, ul = split(U)
             wh, wl = split(W)
@@ -325,7 +325,7 @@
     d_ref[...] = jnp.where(rows_i <= cols_i, d_ref[...], 0.0)
 
 
-B = 256
+B=256
 NT=(((1,),(1,)),((),()))
 NN=(((1,),(0,)),((),()))
 def mm(a,b,dims): return lax.dot_general(a,b,dims,preferred_element_type=F32)
@@ -333,10 +333,10 @@
 def mm3f(a,b,dims):
     ah,al=split(a); bh,bl=split(b)
     return mm3(ah,al,bh,bl,dims)
-
-def factor_solve_kernel(g_ref, p_ref, m_ref, x_ref, y_ref, A, Lh, Ll, mh, ml, d_s, w_s, w_full, gsem):
+def factor_solve_kernel(g_ref, p_ref, m_ref, x_ref, y_ref, A, Lh, Ll, mh, ml, ys, d_s, w_s, e_s, v_s, Wh, Wl, gsem):
     n = p_ref.shape[1]
     nb = n // B
+    h = B // 2
     lens, starts = strips(n)
     copies = [
         pltpu.make_async_copy(
@@ -347,67 +347,102 @@
         for c in range(len(lens))
     ]
     for c in copies: c.start()
-    A[n:n+128, :] = p_ref[...].astype(F32)
-    A[n+128:, :] = jnp.zeros((128, n), F32)
+    A[n:n+h, :] = p_ref[...].astype(F32)
+    A[n+h:, :] = jnp.zeros((A.shape[0]-n-h, n), F32)
+    for r in (Lh, Ll):
+        r[n+B:, :] = jnp.zeros((B, n), BF)
+    ys[...] = jnp.zeros_like(ys)
+    Wh[...] = jnp.zeros_like(Wh); Wl[...] = jnp.zeros_like(Wl)
     mhi, mlo = split(m_ref[...])
     mh[...] = mhi; ml[...] = mlo
-    def blk(i, k): return (pl.ds(pl.multiple_of(i*B, B), B), pl.ds(pl.multiple_of(k*B, B), B))
+    bs = lambda i: pl.ds(pl.multiple_of(i*B, B), B)
     for c in copies: c.wait()
     def step(k, carry):
-        def row_tile(i, _):
-            t = blk(i, k)
-            def inner(j, acc):
-                a, b = blk(i, j), blk(k, j)
-                return acc - mm3(Lh[a], Ll[a], Lh[b], Ll[b], NT)
-            A[t] = lax.fori_loop(0, k, inner, A[t])
-            return 0
-        lax.fori_loop(k, nb+1, row_tile, 0)
+        kp = jnp.maximum(k-1, 0)
+        kn = jnp.minimum(k+1, nb-1)
+        def put(ref, r, c, v): ref[r, c] = v
+        def update(i, c, j):
+            r, cc, jj = bs(i), bs(c), bs(j)
+            v = A[r, cc] - mm3(Lh[r, jj], Ll[r, jj], Lh[cc, jj], Ll[cc, jj], NT)
+            return lambda: put(A, r, cc, v)
+        def panel(i, c):
+            r, cc = bs(i), bs(c)
+            ah, al = split(A[r, cc])
+            hi, lo = split(mm3(ah, al, Wh[...], Wl[...], NT))
+            def fin():
+                Lh[r, cc] = hi; Ll[r, cc] = lo
+            return fin
+        def moment(i, c, dst):
+            r, cc, dd = bs(i), bs(c), bs(dst)
+            v = ys[:, dd] + mm3(mh[:, r], ml[:, r], Lh[r, cc], Ll[r, cc], NN)
+            return lambda: put(ys, slice(None), dd, v)
+        def slot(s):
+            fins = []
+            if s < 8:
+                if s < nb-1:
+                    i = k+1+s
+                    fins.append(panel(jnp.where((k >= 1) & (i <= nb), i, nb+1), kp))
+                if s >= 1:
+                    i = k+s
+                    fins.append(update(jnp.where((k >= 1) & (i <= nb), i, nb+1), k, kp))
+            else:
+                for t in (2*(s-8), 2*(s-8)+1):
+                    ok = (t < (nb-k)*k) & (k+1 < nb)
+                    j = t // (nb-k)
+                    i = k+1 + t - j*(nb-k)
+                    fins.append(update(jnp.where(ok, i, nb+1), kn, jnp.where(ok, j, 0)))
+                i = kp + (s-8)
+                ok = (k >= 1) & (i < nb)
+                fins.append(moment(jnp.where(ok, i, 0), kp, jnp.where(ok, kp, nb)))
+            def fin():
+                for f in fins: f()
+            return fin
         kk = pl.multiple_of(k*B, B)
-        h = 128
         q0, q1 = pl.ds(kk, h), pl.ds(kk+h, h)
+        nx = bs(k+1)
         d_s[...] = A[q0, q0]
-        factor_block(d_s, w_s)
-        w0 = w_s[...]
+        factor_block(d_s, w_s, slot)
+        w0h, w0l = split(w_s[...])
         l00 = d_s[...].T
-        l10 = mm3f(A[q1, q0], w0, NT)
-        d_s[...] = A[q1, q1] - mm3f(l10, l10, NT)
-        factor_block(d_s, w_s)
-        w1 = w_s[...]
-        l11 = d_s[...].T
-        w10 = -mm3f(w1, mm3f(l10, w0, NN), NN)
-        w_full[:h, :h] = w0
-        w_full[:h, h:] = jnp.zeros((h, h), F32)
-        w_full[h:, :h] = w10
-        w_full[h:, h:] = w1
-        for (r, c, v) in ((q0,q0,l00),(q0,q1,jnp.zeros((h,h),F32)),(q1,q0,l10),(q1,q1,l11)):
-            hi, lo = split(v)
-            Lh[r,c]=hi; Ll[r,c]=lo
-        wh, wl = split(w_full[...])
-        def panel(i, _):
-            t = blk(i, k)
-            ah, al = split(A[t])
-            v = mm3(ah, al, wh, wl, NT)
-            hi, lo = split(v)
-            Lh[t] = hi; Ll[t] = lo
-            return 0
-        lax.fori_loop(k+1, nb+1, panel, 0)
-        x_ref[:, pl.ds(kk, B)] = (Lh[n:n+128, pl.ds(kk, B)].astype(F32)+Ll[n:n+128, pl.ds(kk, B)].astype(F32)).astype(BF)
-        def yt(i, acc):
-            a = pl.ds(pl.multiple_of(i*B,B),B)
-            t = blk(i, k)
-            return acc + mm3(mh[:, a], ml[:, a], Lh[t], Ll[t], NN)
-        y_ref[:, pl.ds(kk, B)] = lax.fori_loop(k, nb, yt, jnp.zeros((128, B), F32))
+        a10h, a10l = split(A[q1, q0])
+        l10h, l10l = split(mm3(a10h, a10l, w0h, w0l, NT))
+        e_s[...] = A[q1, q1] - mm3(l10h, l10l, l10h, l10l, NT)
+        nh, nl = split(A[nx, q0])
+        n0h, n0l = split(mm3(nh, nl, w0h, w0l, NT))
+        n1 = A[nx, q1] - mm3(n0h, n0l, l10h, l10l, NT)
+        uh, ul = split(mm3(l10h, l10l, w0h, w0l, NN))
+        factor_block(e_s, v_s, lambda s: slot(s+8))
+        w1h, w1l = split(v_s[...])
+        n1h, n1l = split(n1)
+        n1h, n1l = split(mm3(n1h, n1l, w1h, w1l, NT))
+        Lh[nx, q0] = n0h; Ll[nx, q0] = n0l
+        Lh[nx, q1] = n1h; Ll[nx, q1] = n1l
+        cn = bs(kn)
+        A[nx, cn] = A[nx, cn] - (mm3(n0h, n0l, n0h, n0l, NT) + mm3(n1h, n1l, n1h, n1l, NT))
+        w10h, w10l = split(-mm3(w1h, w1l, uh, ul, NN))
+        z = jnp.zeros((h, h), BF)
+        for W, a, b, c in ((Wh, w0h, w10h, w1h), (Wl, w0l, w10l, w1l)):
+            W[:h, :h] = a; W[h:, :h] = b; W[h:, h:] = c
+        l0, l1 = split(l00), split(e_s[...].T)
+        for L, a, b, c in ((Lh, l0[0], l10h, l1[0]), (Ll, l0[1], l10l, l1[1])):
+            L[q0, q0] = a; L[q0, q1] = z; L[q1, q0] = b; L[q1, q1] = c
+        x_ref[:, bs(kp)] = (Lh[n:n+h, bs(kp)].astype(F32) + Ll[n:n+h, bs(kp)].astype(F32)).astype(BF)
         return carry
     lax.fori_loop(0, nb, step, 0)
+    last = slice(n-B, n)
+    x_ref[:, last] = (Lh[n:n+h, last].astype(F32) + Ll[n:n+h, last].astype(F32)).astype(BF)
+    y_ref[:, :n-B] = ys[:, :n-B]
+    y_ref[:, last] = mm3(mh[:, last], ml[:, last], Lh[last, last], Ll[last, last], NN)
 
 def factor_solve(g, p, m):
     n = p.shape[1]
+    vm = pltpu.VMEM
     return pl.pallas_call(factor_solve_kernel,
         out_shape=[jax.ShapeDtypeStruct((128,n),BF), jax.ShapeDtypeStruct((128,n),F32)],
         in_specs=[pl.BlockSpec(memory_space=pl.ANY), pl.BlockSpec(memory_space=pltpu.VMEM), pl.BlockSpec(memory_space=pltpu.VMEM)],
         out_specs=[pl.BlockSpec(memory_space=pltpu.VMEM)]*2,
-        scratch_shapes=[pltpu.VMEM((n+B,n),F32),pltpu.VMEM((n+B,n),BF),pltpu.VMEM((n+B,n),BF),pltpu.VMEM((128,n),BF),pltpu.VMEM((128,n),BF),
-          pltpu.VMEM((128,128),F32),pltpu.VMEM((128,128),F32),pltpu.VMEM((B,B),F32),pltpu.SemaphoreType.DMA((n//128,))],
+        scratch_shapes=[vm((n+2*B,n),F32),vm((n+2*B,n),BF),vm((n+2*B,n),BF),vm((128,n),BF),vm((128,n),BF),vm((128,n+B),F32),
+          vm((128,128),F32),vm((128,128),F32),vm((128,128),F32),vm((128,128),F32),vm((B,B),BF),vm((B,B),BF),pltpu.SemaphoreType.DMA((n//128,))],
         compiler_params=pltpu.CompilerParams(vmem_limit_bytes=60*2**20),
         name="factor_solve")(g,p,m)
 

time: 293 us -> 265 us (0.904)
  Pallas kernels: 284 us -> 256 us
    pallas_call x1, Pallas kernels: 111 us -> 82.7 us  [factor_solve(): pl.pallas_call(factor_solve_kernel, out_shape=[jax.ShapeDtypeStruct((128,...]
where the time goes in v3:
time: 265 us; the launch traced here: 264 us
  Pallas kernels  256 us (97%)
  local copies, waits for them, and re-layouts  7.62 us (3%)
    pallas_call x1, Pallas kernels, gram_sum(): pl.pallas_call(gram_kernel, out_shape=[jax.ShapeDtypeStruct((2, 6, rows,...  91.9 us
    pallas_call x1, Pallas kernels, factor_solve(): pl.pallas_call(factor_solve_kernel, out_shape=[jax.ShapeDtypeStruct((128,...  82.7 us
    pallas_call x1, Pallas kernels, product_rows(): pl.pallas_call(product_kernel, out_shape=jax.ShapeDtypeStruct((256, n), B...  81.4 us
    unnamed x8, local copies, waits for them, and re-layouts  7.62 us

profile of v3, /device:TPU:1, one launch (start us, length us, event | category | flops | bytes accessed | tf_op | source)
XLA Modules:
  0.0 264.5 jit_solution(5587520377679097837)
XLA Ops:
  0.6 0.0 copy-start.1
  0.6 2.2 copy-done.1
  2.8 0.0 copy-start.2
  2.8 1.0 copy-done.2
  3.9 81.4 %product_rows.1.p_ref = bf16[256,2048]{1,0:T(8,128)(2,1)S(1)} custom-call(bf16[2048,1024]{1,0:T(8,128)(2,1)S(1)} %copy-done.1, bf16[128,2048]{1,0:T(8,128)(2,1)S(1)} %copy-done.2), custom_call_target="tpu_custom_call" | custom-call | tf_op jit(solution)/shard_map/product_rows/pallas_call | solution.py:254
  85.3 91.9 %gram_sum.1 = (f32[2,6,1536,128]{3,2,1,0:T(8,128)S(1)}, bf16[128,2048]{1,0:T(8,128)(2,1)S(1)}) custom-call(bf16[256,2048]{1,0:T(8,128)(2,1)S(1)} %product_rows.1.p_ref), custom_call_target="tpu_custom_call" | custom-call | tf_op jit(solution)/shard_map/gram_sum/pallas_call | solution.py:143
  177.2 0.0 copy-start
  177.2 3.6 %copy-done = f32[2,6,1536,128]{3,2,1,0:T(8,128)} copy-done((f32[2,6,1536,128]{3,2,1,0:T(8,128)}, f32[2,6,1536,128]{3,2,1,0:T(8,128)S(1)}, u32[]{:S(2)}) %copy-start) | copy-done | bytes 9437208
  180.8 0.0 copy-start.3
  180.8 0.8 copy-done.3
  181.6 82.7 %factor_solve.1 = (bf16[128,2048]{1,0:T(8,128)(2,1)}, f32[128,2048]{1,0:T(8,128)}) custom-call(f32[18432,128]{1,0:T(8,128)} %bitcast.1, bf16[128,2048]{1,0:T(8,128)(2,1)} %copy-done.3, f32[128,2048]{1,0:T(8,128)} %m_ref.1), custom_call_target="tpu_custom_call" | custom-call | tf_op jit(solution)/shard_map/factor_solve/pallas_call | solution.py:440
Async XLA Ops:
  0.6 2.2 copy-start.1
  2.8 1.0 copy-start.2
  177.2 3.6 %copy-start = (f32[2,6,1536,128]{3,2,1,0:T(8,128)}, f32[2,6,1536,128]{3,2,1,0:T(8,128)S(1)}, u32[]{:S(2)}) copy-start(f32[2,6,1536,128]{3,2,1,0:T(8,128)S(1)} %get-tuple-element.4) | copy-start | bytes 28311556
  180.8 0.8 copy-start.3
